TPU v7x, 32 devices: a whole 2x2x4 slice. The times are simulated.
32 devices in a mesh: groups: 2 (over y), owner: 4 (over z), tensor: 4 (over x, core).
Axes of the slice: x: 2, y: 2, z: 4, core: 2. Of those that a mesh axis runs over, the one named last changes fastest.
Arguments:
- requests: bfloat16 [384, 8192], P(('groups', 'owner'), 'tensor'), parts along dimension 0, may hold values from -6 to 6
- output_weight: bfloat16 [8192, 8192], P('tensor', 'owner'), may hold values from -0.0625 to 0.0625
- adapter_down_bank: bfloat16 [48, 8192, 64], P(('groups', 'owner'), 'tensor'), parts along dimension 0, may hold values from -0.0625 to 0.0625
- adapter_up_bank: bfloat16 [48, 64, 8192], P(('groups', 'owner'), None, 'tensor'), parts along dimension 0, may hold values from -0.75 to 0.75
- request_adapter: int32 [384], P(('groups', 'owner')), parts along dimension 0, may hold values from 0 to 23, as said below
- adapter_position: int32 [48], P('groups'), parts along dimension 0, may hold values from 0 to 23, as said below
Outputs:
- projected: bfloat16 [384, 8192], P(('groups', 'owner'), 'tensor'), parts along dimension 0
There are 2 independent parts, one for each index of `groups`. A program takes and returns all parts, laid end to end along the dimension named above; an argument that names none is the same for every part. Nothing has to cross between parts.
Inputs may be any that keep to these rules, and one draw needn't show every extreme that they name: `request_adapter`: adapter a sits in bank position adapter_position[a]; position p belongs to owner index p // 6. Among the 48 requests of one owner index (aligned blocks of rows), at most 24 name adapters of one owner; in every draw one owner is named by exactly 24 requests of every block. `adapter_position`: A permutation: each bank position once.
All inputs are finite; a program needn't handle non-finite values.
Results may differ from a plain program's by a relative error of at most 0.005.
Values may be sent and summed in bfloat16 or wider, within the bound.
A program may use at most 64 MiB of HBM per device.

v0:
```python
import jax
import jax.numpy as jnp
from jax import lax
from jax.sharding import PartitionSpec as P


def shards(
    requests, output_weight, adapter_down_bank, adapter_up_bank, request_adapter, adapter_position
):
    rows_dev, features = requests.shape
    owners = lax.axis_size("owner")
    bank_capacity = adapter_down_bank.shape[0]
    most_rows = max(2, (2 * rows_dev + owners - 1) // owners)
    slot_count = owners * most_rows
    gathered = lax.all_gather(requests, "owner", axis=0, tiled=True)
    partial_sum = jnp.dot(gathered, output_weight, preferred_element_type=jnp.float32)
    spread = lax.all_to_all(partial_sum, "owner", split_axis=0, concat_axis=1, tiled=True)
    base_out = lax.psum_scatter(spread, "tensor", scatter_dimension=1, tiled=True)
    adapter_rows = jnp.arange(adapter_position.shape[0], dtype=jnp.int32)
    matched = request_adapter[:, None] == adapter_rows[None, :]
    position = jnp.sum(jnp.where(matched, adapter_position[None, :], 0), axis=1)
    owner_of = position // bank_capacity
    slot_of = position % bank_capacity
    count_rows = owner_of.shape[-1]
    same_owner = owner_of[..., :, None] == owner_of[..., None, :]
    before = jnp.arange(count_rows)[None, :] < jnp.arange(count_rows)[:, None]
    target = owner_of * most_rows + jnp.sum(same_owner & before, axis=-1)
    picker = target[None, :] == jnp.arange(slot_count)[:, None]
    outgoing = jnp.dot(
        picker.astype(jnp.bfloat16), requests, preferred_element_type=jnp.float32
    ).astype(jnp.bfloat16)
    slot_tags = jnp.sum(jnp.where(picker, slot_of[None, :] + 1, 0), axis=1)
    received_rows, arrived_tags = (
        lax.all_to_all(
            outgoing.reshape(owners, most_rows, features),
            "owner",
            split_axis=0,
            concat_axis=0,
            tiled=True,
        ),
        lax.all_to_all(
            slot_tags.reshape(owners, most_rows), "owner", split_axis=0, concat_axis=0, tiled=True
        ),
    )
    received_rows = received_rows.reshape(slot_count, features)
    arrived_tags = arrived_tags.reshape(slot_count)
    select = arrived_tags[:, None] == jnp.arange(1, bank_capacity + 1)[None, :]
    complete_low_rank = jnp.einsum(
        "jw,bwo->jbo", received_rows, adapter_down_bank, preferred_element_type=jnp.float32
    )
    partial_low = jnp.sum(jnp.where(select[:, :, None], complete_low_rank, 0.0), axis=1)
    summed = lax.psum(partial_low, "tensor").astype(jnp.bfloat16)
    scattered_low_rank = jnp.where(
        select[:, :, None], summed[:, None, :], jnp.zeros((), jnp.bfloat16)
    )
    delta_rows = jnp.einsum(
        "vtj,tje->ve", scattered_low_rank, adapter_up_bank, preferred_element_type=jnp.float32
    ).astype(jnp.bfloat16)
    returned_rows = lax.all_to_all(
        delta_rows.reshape(owners, most_rows, delta_rows.shape[1]),
        "owner",
        split_axis=0,
        concat_axis=0,
        tiled=True,
    )
    returned_rows = returned_rows.reshape(slot_count, delta_rows.shape[1])
    own_delta = jnp.dot(
        picker.T.astype(jnp.bfloat16), returned_rows, preferred_element_type=jnp.float32
    )
    return (base_out + own_delta).astype(jnp.bfloat16)


def solution(mesh):
    placed = (
        P(("groups", "owner"), "tensor"),
        P("tensor", "owner"),
        P(("groups", "owner"), "tensor", None),
        P(("groups", "owner"), None, "tensor"),
        P(("groups", "owner")),
        P("groups"),
    )
    return jax.shard_map(
        shards,
        mesh=mesh,
        in_specs=placed,
        out_specs=P(("groups", "owner"), "tensor"),
        check_vma=False,
    )
```

profile of v0, /device:TPU:6, one launch (start us, length us, event | category | flops | bytes accessed | tf_op | source)
XLA Modules:
  0.0 129.3 jit_solution(8577265137441582588)
XLA Ops:
  6.5 0.0 copy-start
  6.5 0.0 reduce-scatter.2.cloned.1.call-start
  6.5 20.2 %all_gather.3 = bf16[192,2048]{1,0:T(8,128)(2,1)S(1)} all-gather(bf16[48,2048]{1,0:T(8,128)(2,1)} %param.6), channel_id=1, replica_groups=mesh['groups'=2,'owner'=4,'tensor'=4] {'owner'}, dimensions={0}, use_global_device_ids=true | all-gather | bytes 983040 | tf_op jit(solution)/shard_map/all_gather | solution.py:15
  26.7 5.2 %fusion.11 = f32[192,2048]{1,0:T(8,128)S(1)} fusion(bf16[192,2048]{1,0:T(8,128)(2,1)S(1)} %all_gather.3, bf16[2048,2048]{1,0:T(8,128)(2,1)} %param.7), kind=kOutput, calls=%fused_computation.26 | convolution fusion | flops 1610612736 | bytes 10747904 | tf_op jit(solution)/shard_map/dot_general | solution.py:16
  31.9 38.4 %all_to_all.38 = f32[4,48,2048]{2,1,0:T(8,128)S(1)} all-to-all(f32[4,48,2048]{2,1,0:T(8,128)S(1)} %bitcast.27), channel_id=1, replica_groups=mesh['groups'=2,'owner'=4,'tensor'=4] {'owner'}, dimensions={0} | all-to-all | bytes 3145728 | tf_op jit(solution)/shard_map/all_to_all | solution.py:17
  70.3 1.3 copy.12
  71.6 0.0 copy-start.3
  71.6 0.0 copy-start.4
  71.6 0.0 reduce-scatter.2.cloned.1.call-update
  71.6 0.6 copy-done.3
  72.3 0.0 copy-done.4
  72.3 0.1 select_reduce_fusion.2
  72.4 0.2 convert_reduce_fusion
  72.6 0.1 select_reduce_fusion.1
  72.7 0.7 all_to_all.30
  73.3 3.2 %all-to-all-start.1 = ((s32[4,1,24]{2,1,0:T(1,128)}), s32[4,1,24]{2,1,0:T(1,128)S(1)}, u32[]{:S(2)}, u32[]{:S(2)}) async-start(s32[4,1,24]{2,1,0:T(1,128)} %bitcast.2), calls=%async_computation.2 | async-start | bytes 4096 | tf_op jit(solution)/shard_map/all_to_all | solution.py:41
  76.6 0.0 copy-done.2
  76.6 1.1 convolution_convert_fusion
  77.7 4.3 %all-to-all-done.1 = s32[4,1,24]{2,1,0:T(1,128)S(1)} async-done(((s32[4,1,24]{2,1,0:T(1,128)}), s32[4,1,24]{2,1,0:T(1,128)S(1)}, u32[]{:S(2)}, u32[]{:S(2)}) %all-to-all-start.1) | async-done | bytes 416 | tf_op jit(solution)/shard_map/all_to_all | solution.py:41
  82.0 3.6 %all-to-all-start.2 = ((bf16[4,24,2048]{2,1,0:T(8,128)(2,1)}), bf16[4,24,2048]{2,1,0:T(8,128)(2,1)S(1)}, u32[]{:S(2)}, u32[]{:S(2)}) async-start(bf16[4,24,2048]{2,1,0:T(8,128)(2,1)} %bitcast.3), calls=%async_computation.3 | async-start | bytes 786432 | tf_op jit(solution)/shard_map/all_to_all | solution.py:34
  85.6 0.5 broadcast.118
  86.1 0.7 reduce.3
  86.8 0.1 eq.69
  86.9 0.1 broadcast_compare_fusion
  87.0 8.0 %all-to-all-done.2 = bf16[4,24,2048]{2,1,0:T(8,128)(2,1)S(1)} async-done(((bf16[4,24,2048]{2,1,0:T(8,128)(2,1)}), bf16[4,24,2048]{2,1,0:T(8,128)(2,1)S(1)}, u32[]{:S(2)}, u32[]{:S(2)}) %all-to-all-start.2) | async-done | bytes 393248 | tf_op jit(solution)/shard_map/all_to_all | solution.py:34
  95.0 0.0 copy-done
  95.0 0.6 fusion.12
  95.6 10.4 %psum.7 = bf16[96,64]{0,1:T(8,128)(2,1)S(1)} all-reduce(f32[96,64]{0,1:T(8,128)S(1)} %select_reduce_fusion), channel_id=1, replica_groups=mesh['groups'=2,'owner'=4,'tensor'=4] {'tensor'}, use_global_device_ids=true, to_apply=%region_5.6 | all-reduce | flops 6144 | bytes 36864 | tf_op jit(solution)/shard_map/psum | solution.py:52
  106.0 0.0 copy-done.1
  106.0 0.4 fusion
  106.5 14.1 %all_to_all.39 = bf16[4,24,2048]{2,1,0:T(8,128)(2,1)S(1)} all-to-all(bf16[4,24,2048]{2,1,0:T(8,128)(2,1)S(1)} %bitcast.29), channel_id=1, replica_groups=mesh['groups'=2,'owner'=4,'tensor'=4] {'owner'}, dimensions={0} | all-to-all | bytes 786432 | tf_op jit(solution)/shard_map/all_to_all | solution.py:59
  120.6 1.9 %fusion.1 = bf16[48,2048]{1,0:T(8,128)(2,1)} fusion(f32[48,2048]{1,0:T(8,128)} %reduce-scatter.2.cloned.1.call-done, bf16[96,2048]{1,0:T(8,128)(2,1)S(1)} %bitcast.28, s32[48]{0:T(128)S(1)} %multiply_add_fusion), kind=kOutput, calls=%fused_computation.4 | convolution fusion | flops 19075584 | bytes 983232 | tf_op jit(solution)/shard_map/dot_general | solution.py:67
  (7 shorter events, 0.1 us)
Async XLA Ops:
  6.5 88.5 %copy-start = (bf16[6,2048,64]{1,2,0:T(8,128)(2,1)S(1)}, bf16[6,2048,64]{1,2,0:T(8,128)(2,1)}, u32[]{:S(2)}) copy-start(bf16[6,2048,64]{1,2,0:T(8,128)(2,1)} %param.8) | copy-start | bytes 4718596
  6.5 114.0 %reduce-scatter.2.cloned.1.call-start = ((), (), s32[]{:S(2)}) async-start(), calls=%async_computation.5 | async-start | bytes 1966080 | tf_op jit(solution)/shard_map/reduce_scatter | solution.py:18
  71.6 0.7 copy-start.3
  71.6 0.7 copy-start.4
  71.6 5.0 %copy-start.2 = (bf16[48,2048]{1,0:T(8,128)(2,1)S(1)}, bf16[48,2048]{1,0:T(8,128)(2,1)}, u32[]{:S(2)}) copy-start(bf16[48,2048]{1,0:T(8,128)(2,1)} %param.6) | copy-start | bytes 589828
  73.3 8.7 %all-to-all-start.1 = ((s32[4,1,24]{2,1,0:T(1,128)}), s32[4,1,24]{2,1,0:T(1,128)S(1)}, u32[]{:S(2)}, u32[]{:S(2)}) async-start(s32[4,1,24]{2,1,0:T(1,128)} %bitcast.2), calls=%async_computation.2 | async-start | bytes 4096 | tf_op jit(solution)/shard_map/all_to_all | solution.py:41
  82.0 24.0 %copy-start.1 = (bf16[6,64,2048]{2,1,0:T(8,128)(2,1)S(1)}, bf16[6,64,2048]{2,1,0:T(8,128)(2,1)}, u32[]{:S(2)}) copy-start(bf16[6,64,2048]{2,1,0:T(8,128)(2,1)} %param.9) | copy-start | bytes 4718596
  82.0 13.0 %all-to-all-start.2 = ((bf16[4,24,2048]{2,1,0:T(8,128)(2,1)}), bf16[4,24,2048]{2,1,0:T(8,128)(2,1)S(1)}, u32[]{:S(2)}, u32[]{:S(2)}) async-start(bf16[4,24,2048]{2,1,0:T(8,128)(2,1)} %bitcast.3), calls=%async_computation.3 | async-start | bytes 786432 | tf_op jit(solution)/shard_map/all_to_all | solution.py:34
Sparse Core Ops, SparseCore 0:
  71.8 26.2 reduce-scatter.1
where the time goes:
time: 132 us; the launch traced here: 129 us
  blocking collectives  83.1 us (63%)
  between operations  13.5 us (10%)
  waiting for transfers between devices  12.3 us (9%)
  matrix products  9.26 us (7%)
  starting transfers between devices  6.82 us (5%)
  local copies, waits for them, and re-layouts  3.18 us (2%)
    all_to_all x1, blocking collectives, shards(): lax.all_to_all(partial_sum, 'owner', split_axis=0, concat_axis=1, tiled=T...  38.4 us
    all_gather x1, blocking collectives, shards(): gathered = lax.all_gather(requests, 'owner', axis=0, tiled=True)  20.2 us
    all_to_all x1, blocking collectives, shards(): lax.all_to_all(delta_rows.reshape(owners, most_rows, delta_rows.shape[1])...  14.1 us
    psum x1, blocking collectives, shards(): summed = lax.psum(partial_low, 'tensor').astype(jnp.bfloat16)  10.4 us
    all_to_all x1, waiting for transfers between devices, shards(): lax.all_to_all(outgoing.reshape(owners, most_rows, features), 'owner', sp...  8.03 us
    dot_general x1, matrix products, shards(): jnp.dot(gathered, output_weight, preferred_element_type=jnp.float32)  5.19 us
    all_to_all x1, waiting for transfers between devices, shards(): lax.all_to_all(slot_tags.reshape(owners, most_rows), 'owner', split_axis=...  4.28 us
    all_to_all x1, starting transfers between devices, shards(): lax.all_to_all(outgoing.reshape(owners, most_rows, features), 'owner', sp...  3.59 us
  transfers between devices with their start and end apart: 3, of which 2 were waited for; matrix products, arithmetic and copies ran while one was open for 3% of the time, Pallas kernels for 0%

commit v1 on v0

--- a/solution.py
+++ b/solution.py
@@ -1,10 +1,14 @@
+import functools
+
 import jax
 import jax.numpy as jnp
 from jax import lax
+from jax.experimental import pallas as pl
+from jax.experimental.pallas import tpu as pltpu
 from jax.sharding import PartitionSpec as P
 
 
-def shards(
+def general(
     requests, output_weight, adapter_down_bank, adapter_up_bank, request_adapter, adapter_position
 ):
     rows_dev, features = requests.shape
@@ -70,6 +74,303 @@
     return (base_out + own_delta).astype(jnp.bfloat16)
 
 
+MESH = pl.DeviceIdType.MESH
+F32, BF16 = jnp.float32, jnp.bfloat16
+LANES = 128
+
+
+def dot(a, b, dims=((1,), (0,))):
+    return lax.dot_general(a, b, (dims, ((), ())), preferred_element_type=F32)
+
+
+def kernel(
+    n, bank, rank, cap, tile,
+    x_hbm, meta_hbm, w_hbm, down_hbm, up_hbm, out_ref,
+    xg, w, down, up, low, part, parts_in, acc, swap, swap_in, delta_out, delta_in,
+    local_sem, up_send, dn_send, x_recv, low_send, low_recv, rs_send, rs_recv,
+    delta_send, delta_recv, swap_send, swap_recv,
+):
+    g, o, t = lax.axis_index("groups"), lax.axis_index("owner"), lax.axis_index("tensor")
+    rows, width = x_hbm.shape
+    cols = w.shape[1]
+    half = cols // 2
+    copies = bank * rank // LANES
+
+    def local(src, dst, i):
+        return pltpu.make_async_copy(src, dst, local_sem.at[i])
+
+    loads = [
+        local(x_hbm, xg.at[o, :, pl.ds(0, width)], 0),
+        local(meta_hbm, xg.at[o, :, pl.ds(width, 2 * LANES)], 1),
+        local(down_hbm, down, 2),
+        local(w_hbm, w, 3),
+        local(up_hbm, up, 4),
+    ]
+    for load in loads:
+        load.start()
+
+    barrier = pltpu.get_barrier_semaphore()
+    for s in range(1, n):
+        pl.semaphore_signal(barrier, inc=1, device_id=(g, lax.rem(o + s, n), t), device_id_type=MESH)
+        pl.semaphore_signal(barrier, inc=1, device_id=(g, o, lax.rem(t + s, n)), device_id_type=MESH)
+
+    @pl.when(o != t)
+    def _():
+        pl.semaphore_signal(barrier, inc=1, device_id=(g, t, o), device_id_type=MESH)
+
+    pl.semaphore_wait(barrier, 2 * (n - 1) + jnp.where(o != t, 1, 0))
+    loads[0].wait()
+    loads[1].wait()
+
+    def remote(src, dst, send, recv, device):
+        return pltpu.make_async_remote_copy(
+            src_ref=src, dst_ref=dst, send_sem=send, recv_sem=recv, device_id=device, device_id_type=MESH
+        )
+
+    def x_up(b):
+        return remote(xg.at[b], xg.at[b], up_send.at[b], x_recv.at[b], (g, jnp.minimum(o + 1, n - 1), t))
+
+    def x_down(b):
+        return remote(xg.at[b], xg.at[b], dn_send.at[b], x_recv.at[b], (g, jnp.maximum(o - 1, 0), t))
+
+    def low_copy(b, to, src):
+        return remote(low.at[b, src], low.at[b, src], low_send.at[b, to], low_recv.at[b, src], (g, o, to))
+
+    def part_copy(b, src):
+        return remote(part.at[b], parts_in.at[src], rs_send.at[b], rs_recv.at[src], (g, o, b))
+
+    def delta_copy(b, src):
+        return remote(
+            delta_out.at[b], delta_in.at[pl.ds(src * 2 * cap, 2 * cap)], delta_send.at[b], delta_recv.at[src], (g, b, t)
+        )
+
+    def swap_copy():
+        return remote(swap, swap_in, swap_send, swap_recv, (g, t, o))
+
+    mirrored = 2 * o >= n
+    near = jnp.where(mirrored, n - 1 - o, o)
+
+    def order(k):
+        inner = jnp.where(k % 2 == 1, near - (k + 1) // 2, near + k // 2)
+        b = jnp.where(k <= 2 * near, inner, k)
+        return jnp.where(mirrored, n - 1 - b, b)
+
+    def finish_parts():
+        for s in range(1, n):
+            part_copy(t, lax.rem(t + s, n)).wait_recv()
+
+        @pl.loop(0, cols // tile)
+        def _(c):
+            at = pl.ds(pl.multiple_of(c * tile, tile), tile)
+            total = acc[:, at]
+            for s in range(1, n):
+                total += parts_in[lax.rem(t + s, n), :, at].astype(F32)
+            acc[:, at] = total
+            swap[:, at] = total.astype(BF16)
+
+        @pl.when(o != t)
+        def _():
+            swap_copy().start()
+
+    def block(k, carry):
+        b = order(k)
+
+        @pl.when(k > 0)
+        def _():
+            x_up(b).wait_recv()
+
+        @pl.when((o < n - 1) & (b <= o))
+        def _():
+            x_up(b).start()
+
+        @pl.when((o > 0) & (b >= o))
+        def _():
+            x_down(b).start()
+
+        @pl.when(k == 0)
+        def _():
+            loads[2].wait()
+
+        place = xg[b, :, width : width + LANES].astype(F32)
+        target = xg[b, :, width + LANES : width + 2 * LANES].astype(F32)
+        lane = lax.broadcasted_iota(jnp.int32, (rows, bank * rank), 1)
+        mine = jnp.concatenate([place] * copies, axis=1) == (lane // rank + o * bank).astype(F32)
+        every = jnp.where(mine, dot(xg[b, :, :width], down[...], ((1,), (1,))), 0.0)
+        folded = every[:, :LANES]
+        for i in range(1, copies):
+            folded += every[:, i * LANES : (i + 1) * LANES]
+        low[b, t] = folded + pltpu.roll(folded, rank, 1)
+        for s in range(1, n):
+            low_copy(b, lax.rem(t + s, n), t).start()
+
+        @pl.when(k == 0)
+        def _():
+            loads[3].wait()
+
+        @pl.loop(0, cols // tile)
+        def _(c):
+            at = pl.ds(pl.multiple_of(c * tile, tile), tile)
+            value = dot(xg[b, :, :width], w[:, at])
+            part[b, :, at] = value.astype(BF16)
+
+            @pl.when(b == t)
+            def _():
+                acc[:, at] = value
+
+        @pl.when(b != t)
+        def _():
+            part_copy(b, t).start()
+
+        @pl.when(k == 0)
+        def _():
+            loads[4].wait()
+
+        for s in range(1, n):
+            low_copy(b, t, lax.rem(t + s, n)).wait_recv()
+        total = low[b, 0]
+        for s in range(1, n):
+            total += low[b, s]
+        spread = jnp.where(mine, jnp.concatenate([total] * copies, axis=1), 0.0).astype(BF16)
+        slot = lax.broadcasted_iota(jnp.int32, (rows, LANES), 1)
+        picker = (target == (slot + o * cap).astype(F32)) & (slot < cap)
+        packed = dot(picker.astype(F32).astype(BF16), spread, ((0,), (0,)))[:cap].astype(BF16)
+        made = jnp.concatenate([dot(packed, up[:, :half]), dot(packed, up[:, half:])], axis=0).astype(BF16)
+
+        @pl.when(b == o)
+        def _():
+            delta_in[pl.ds(pl.multiple_of(o * 2 * cap, 2 * cap), 2 * cap), :] = made
+
+        @pl.when(b != o)
+        def _():
+            delta_out[b] = made
+            delta_copy(b, o).start()
+
+        @pl.when((k > 0) & (order(jnp.maximum(k - 1, 0)) == t))
+        def _():
+            finish_parts()
+
+        return carry
+
+    lax.fori_loop(0, n, block, 0)
+
+    @pl.when(order(n - 1) == t)
+    def _():
+        finish_parts()
+
+    for s in range(1, n):
+        delta_copy(o, lax.rem(o + s, n)).wait_recv()
+
+    @pl.when(o != t)
+    def _():
+        swap_copy().wait_recv()
+        acc[...] = swap_in[...].astype(F32)
+
+    target = xg[o, :, width + LANES : width + LANES + 1].astype(F32).astype(jnp.int32)
+    wanted = target + target // cap * cap
+    slot = lax.broadcasted_iota(jnp.int32, (rows, n * 2 * cap), 1)
+    for h in range(2):
+        unpick = (slot == wanted + h * cap).astype(F32).astype(BF16)
+        at = slice(h * half, (h + 1) * half)
+        out_ref[:, at] = (acc[:, at] + dot(unpick, delta_in[...])).astype(BF16)
+
+    def drain(b, carry):
+        @pl.when((o < n - 1) & (b <= o))
+        def _():
+            x_up(b).wait_send()
+
+        @pl.when((o > 0) & (b >= o))
+        def _():
+            x_down(b).wait_send()
+
+        @pl.when(b != t)
+        def _():
+            part_copy(b, t).wait_send()
+
+        @pl.when(b != o)
+        def _():
+            delta_copy(b, o).wait_send()
+
+        for s in range(1, n):
+            low_copy(b, lax.rem(t + s, n), t).wait_send()
+        return carry
+
+    lax.fori_loop(0, n, drain, 0)
+
+    @pl.when(o != t)
+    def _():
+        swap_copy().wait_send()
+
+
+def fused(
+    requests, output_weight, adapter_down_bank, adapter_up_bank, request_adapter, adapter_position
+):
+    rows, width = requests.shape
+    n = lax.axis_size("owner")
+    cols = output_weight.shape[1]
+    bank, rank = adapter_down_bank.shape[0], adapter_down_bank.shape[2]
+    cap = max(2, (2 * rows + n - 1) // n)
+    adapters = jnp.arange(adapter_position.shape[0], dtype=jnp.int32)
+    matched = request_adapter[:, None] == adapters[None, :]
+    position = jnp.sum(jnp.where(matched, adapter_position[None, :], 0), axis=1)
+    owner_of = position // bank
+    before = jnp.arange(rows)[None, :] < jnp.arange(rows)[:, None]
+    same = owner_of[:, None] == owner_of[None, :]
+    target = owner_of * cap + jnp.sum(same & before, axis=-1)
+    meta = jnp.where(jnp.arange(2 * LANES)[None, :] < LANES, position[:, None], target[:, None]).astype(BF16)
+    down = jnp.swapaxes(adapter_down_bank, 1, 2).reshape(bank * rank, width)
+    up = adapter_up_bank.reshape(bank * rank, cols)
+    anywhere = pl.BlockSpec(memory_space=pl.ANY)
+    dma = pltpu.SemaphoreType.DMA
+    return pl.pallas_call(
+        functools.partial(kernel, n, bank, rank, cap, 512),
+        out_shape=jax.ShapeDtypeStruct((rows, cols), BF16),
+        in_specs=[anywhere] * 5,
+        out_specs=pl.BlockSpec(memory_space=pltpu.VMEM),
+        scratch_shapes=[
+            pltpu.VMEM((n, rows, width + 2 * LANES), BF16),
+            pltpu.VMEM((width, cols), BF16),
+            pltpu.VMEM((bank * rank, width), BF16),
+            pltpu.VMEM((bank * rank, cols), BF16),
+            pltpu.VMEM((n, n, rows, LANES), F32),
+            pltpu.VMEM((n, rows, cols), BF16),
+            pltpu.VMEM((n, rows, cols), BF16),
+            pltpu.VMEM((rows, cols), F32),
+            pltpu.VMEM((rows, cols), BF16),
+            pltpu.VMEM((rows, cols), BF16),
+            pltpu.VMEM((n, 2 * cap, cols // 2), BF16),
+            pltpu.VMEM((n * 2 * cap, cols // 2), BF16),
+            dma((5,)), dma((n,)), dma((n,)), dma((n,)), dma((n, n)), dma((n, n)), dma((n,)), dma((n,)),
+            dma((n,)), dma((n,)), dma, dma,
+        ],
+        compiler_params=pltpu.CompilerParams(
+            collective_id=0, has_side_effects=True, vmem_limit_bytes=60 * 2**20
+        ),
+    )(requests, meta, output_weight, down, up)
+
+
+def shards(
+    requests, output_weight, adapter_down_bank, adapter_up_bank, request_adapter, adapter_position
+):
+    arguments = (
+        requests, output_weight, adapter_down_bank, adapter_up_bank, request_adapter, adapter_position
+    )
+    rows, width = requests.shape
+    owners, pieces = lax.axis_size("owner"), lax.axis_size("tensor")
+    bank, rank = adapter_down_bank.shape[0], adapter_down_bank.shape[2]
+    cap = max(2, (2 * rows + owners - 1) // owners)
+    fits = (
+        owners == pieces
+        and output_weight.shape[1] % 512 == 0
+        and 2 * rank == LANES
+        and bank * rank % LANES == 0
+        and rows % 16 == 0
+        and cap % 8 == 0
+        and cap <= LANES
+        and owners * max(bank, cap) <= 256
+    )
+    return fused(*arguments) if fits else general(*arguments)
+
+
 def solution(mesh):
     placed = (
         P(("groups", "owner"), "tensor"),

time: 132 us -> 52 us (0.39)
  the two profiles are of different devices: /device:TPU:6 before, /device:TPU:7 now
where the time goes in v1:
time: 52 us; the launch traced here: 51.8 us
  Pallas kernels  48.5 us (93%)
  other arithmetic  1.67 us (3%)
  local copies, waits for them, and re-layouts  1.62 us (3%)
    pallas_call x1, Pallas kernels, fused(): pl.pallas_call(functools.partial(kernel, n, bank, rank, cap, 512), out_sh...  48.5 us
    unnamed x1, local copies, waits for them, and re-layouts  1.62 us

profile of v1, /device:TPU:7, one launch (start us, length us, event | category | flops | bytes accessed | tf_op | source)
XLA Modules:
  0.0 51.8 jit_solution(8816869185625792175)
XLA Ops:
  0.0 0.8 %select_reduce_fusion = s32[48]{0:T(128)S(1)} fusion(s32[24]{0:T(128)} %param.11, s32[48]{0:T(128)} %param.10), kind=kLoop, calls=%fused_computation.4 | loop fusion | flops 3408 | bytes 480 | tf_op jit(solution)/shard_map/reduce_sum | solution.py:314
  0.8 0.2 convert_reduce_fusion
  1.0 0.7 %select_convert_fusion.meta_hbm = bf16[48,256]{1,0:T(8,128)(2,1)} fusion(s32[48]{0:T(128)S(1)} %multiply_add_fusion, s32[48]{0:T(128)S(1)} %select_reduce_fusion, pred[256]{0:T(512)(128)(4,1)S(1)} %iota_compare_fusion.2), kind=kLoop, calls=%fused_computation | loop fusion | flops 24576 | bytes 25216 | tf_op jit(solution)/shard_map/convert_element_type | solution.py:319
  1.7 48.5 %shard_map.64 = bf16[48,2048]{1,0:T(8,128)(2,1)} custom-call(bf16[48,2048]{1,0:T(8,128)(2,1)} %x_hbm.1, bf16[48,256]{1,0:T(8,128)(2,1)} %select_convert_fusion.meta_hbm, bf16[2048,2048]{1,0:T(8,128)(2,1)} %w_hbm.1, bf16[384,2048]{1,0:T(8,128)(2,1)} %bitcast.4, bf16[384,2048]{1,0:T(8,128)(2,1)} %bitcast.5), custom_call_target="tpu_custom_call" | custom-call | tf_op jit(solution)/shard_map/pallas_call | solution.py:324
  50.2 1.6 %copy.8 = bf16[48,2048]{1,0:T(8,128)(2,1)} copy(bf16[48,2048]{1,0:T(8,128)(2,1)} %shard_map.64) | data formatting | bytes 393216
  (3 shorter events, 0.0 us)

commit v2 on v1

--- a/solution.py
+++ b/solution.py
@@ -85,7 +85,7 @@
 
 def kernel(
     n, bank, rank, cap, tile,
-    x_hbm, meta_hbm, w_hbm, down_hbm, up_hbm, out_ref,
+    x_hbm, named_ref, place_ref, w_hbm, down_hbm, up_hbm, out_ref,
     xg, w, down, up, low, part, parts_in, acc, swap, swap_in, delta_out, delta_in,
     local_sem, up_send, dn_send, x_recv, low_send, low_recv, rs_send, rs_recv,
     delta_send, delta_recv, swap_send, swap_recv,
@@ -101,10 +101,9 @@
 
     loads = [
         local(x_hbm, xg.at[o, :, pl.ds(0, width)], 0),
-        local(meta_hbm, xg.at[o, :, pl.ds(width, 2 * LANES)], 1),
-        local(down_hbm, down, 2),
-        local(w_hbm, w, 3),
-        local(up_hbm, up, 4),
+        local(down_hbm, down, 1),
+        local(w_hbm, w, 2),
+        local(up_hbm, up, 3),
     ]
     for load in loads:
         load.start()
@@ -118,9 +117,21 @@
     def _():
         pl.semaphore_signal(barrier, inc=1, device_id=(g, t, o), device_id_type=MESH)
 
+    down_rows = lax.broadcasted_iota(jnp.int32, (rows, rows), 0)
+    across = lax.broadcasted_iota(jnp.int32, (rows, rows), 1)
+    same_row = down_rows == across
+    named = jnp.sum(jnp.where(same_row, named_ref[...].astype(F32), 0.0), axis=1, keepdims=True)
+    adapters = lax.broadcasted_iota(jnp.int32, (rows, place_ref.shape[1]), 1).astype(F32)
+    places = jnp.sum(jnp.where(named == adapters, place_ref[...].astype(F32), 0.0), axis=1, keepdims=True)
+    holder = sum(jnp.where(places >= float(i * bank), 1.0, 0.0) for i in range(1, n))
+    holder_row = jnp.sum(jnp.where(same_row, holder, 0.0), axis=0, keepdims=True)
+    earlier = jnp.sum(jnp.where((holder == holder_row) & (across < down_rows), 1.0, 0.0), axis=1, keepdims=True)
+    targets = holder * cap + earlier
+    wide = (rows, LANES)
+    xg[o, :, width : width + LANES] = jnp.broadcast_to(places, wide).astype(BF16)
+    xg[o, :, width + LANES : width + 2 * LANES] = jnp.broadcast_to(targets, wide).astype(BF16)
     pl.semaphore_wait(barrier, 2 * (n - 1) + jnp.where(o != t, 1, 0))
     loads[0].wait()
-    loads[1].wait()
 
     def remote(src, dst, send, recv, device):
         return pltpu.make_async_remote_copy(
@@ -136,16 +147,16 @@
     def low_copy(b, to, src):
         return remote(low.at[b, src], low.at[b, src], low_send.at[b, to], low_recv.at[b, src], (g, o, to))
 
-    def part_copy(b, src):
-        return remote(part.at[b], parts_in.at[src], rs_send.at[b], rs_recv.at[src], (g, o, b))
+    def part_copy(b, src, h):
+        return remote(part.at[b, h], parts_in.at[src, h], rs_send.at[b, h], rs_recv.at[src, h], (g, o, b))
 
     def delta_copy(b, src):
         return remote(
             delta_out.at[b], delta_in.at[pl.ds(src * 2 * cap, 2 * cap)], delta_send.at[b], delta_recv.at[src], (g, b, t)
         )
 
-    def swap_copy():
-        return remote(swap, swap_in, swap_send, swap_recv, (g, t, o))
+    def swap_copy(h):
+        return remote(swap.at[h], swap_in.at[h], swap_send.at[h], swap_recv.at[h], (g, t, o))
 
     mirrored = 2 * o >= n
     near = jnp.where(mirrored, n - 1 - o, o)
@@ -156,40 +167,43 @@
         return jnp.where(mirrored, n - 1 - b, b)
 
     def finish_parts():
-        for s in range(1, n):
-            part_copy(t, lax.rem(t + s, n)).wait_recv()
-
-        @pl.loop(0, cols // tile)
-        def _(c):
-            at = pl.ds(pl.multiple_of(c * tile, tile), tile)
-            total = acc[:, at]
+        for h in range(2):
             for s in range(1, n):
-                total += parts_in[lax.rem(t + s, n), :, at].astype(F32)
-            acc[:, at] = total
-            swap[:, at] = total.astype(BF16)
-
-        @pl.when(o != t)
-        def _():
-            swap_copy().start()
+                part_copy(t, lax.rem(t + s, n), h).wait_recv()
+            total = acc[h]
+            for s in range(1, n):
+                total += parts_in[lax.rem(t + s, n), h].astype(F32)
+            acc[h] = total
+            swap[h] = total.astype(BF16)
+
+            @pl.when(o != t)
+            def _():
+                swap_copy(h).start()
 
     def block(k, carry):
         b = order(k)
 
-        @pl.when(k > 0)
-        def _():
-            x_up(b).wait_recv()
-
-        @pl.when((o < n - 1) & (b <= o))
-        def _():
-            x_up(b).start()
-
-        @pl.when((o > 0) & (b >= o))
-        def _():
-            x_down(b).start()
+        below, above = jnp.maximum(o - k, 0), jnp.minimum(o + k, n - 1)
+
+        @pl.when((k > 0) & (o - k >= 0))
+        def _():
+            x_up(below).wait_recv()
+
+        @pl.when((o < n - 1) & (o - k >= 0))
+        def _():
+            x_up(below).start()
+
+        @pl.when((k > 0) & (o + k < n))
+        def _():
+            x_up(above).wait_recv()
+
+        @pl.when((o > 0) & (o + k < n))
+        def _():
+            x_down(above).start()
 
         @pl.when(k == 0)
         def _():
-            loads[2].wait()
+            loads[1].wait()
 
         place = xg[b, :, width : width + LANES].astype(F32)
         target = xg[b, :, width + LANES : width + 2 * LANES].astype(F32)
@@ -205,25 +219,27 @@
 
         @pl.when(k == 0)
         def _():
+            loads[2].wait()
+
+        for h in range(2):
+
+            @pl.loop(0, half // tile)
+            def _(c):
+                at = pl.ds(pl.multiple_of(c * tile, tile), tile)
+                value = dot(xg[b, :, :width], w[:, pl.ds(pl.multiple_of(h * half + c * tile, tile), tile)])
+                part[b, h, :, at] = value.astype(BF16)
+
+                @pl.when(b == t)
+                def _():
+                    acc[h, :, at] = value
+
+            @pl.when(b != t)
+            def _():
+                part_copy(b, t, h).start()
+
+        @pl.when(k == 0)
+        def _():
             loads[3].wait()
-
-        @pl.loop(0, cols // tile)
-        def _(c):
-            at = pl.ds(pl.multiple_of(c * tile, tile), tile)
-            value = dot(xg[b, :, :width], w[:, at])
-            part[b, :, at] = value.astype(BF16)
-
-            @pl.when(b == t)
-            def _():
-                acc[:, at] = value
-
-        @pl.when(b != t)
-        def _():
-            part_copy(b, t).start()
-
-        @pl.when(k == 0)
-        def _():
-            loads[4].wait()
 
         for s in range(1, n):
             low_copy(b, t, lax.rem(t + s, n)).wait_recv()
@@ -260,18 +276,19 @@
     for s in range(1, n):
         delta_copy(o, lax.rem(o + s, n)).wait_recv()
 
-    @pl.when(o != t)
-    def _():
-        swap_copy().wait_recv()
-        acc[...] = swap_in[...].astype(F32)
-
     target = xg[o, :, width + LANES : width + LANES + 1].astype(F32).astype(jnp.int32)
     wanted = target + target // cap * cap
     slot = lax.broadcasted_iota(jnp.int32, (rows, n * 2 * cap), 1)
     for h in range(2):
         unpick = (slot == wanted + h * cap).astype(F32).astype(BF16)
-        at = slice(h * half, (h + 1) * half)
-        out_ref[:, at] = (acc[:, at] + dot(unpick, delta_in[...])).astype(BF16)
+        own = dot(unpick, delta_in[...])
+
+        @pl.when(o != t)
+        def _():
+            swap_copy(h).wait_recv()
+            acc[h] = swap_in[h].astype(F32)
+
+        out_ref[:, h * half : (h + 1) * half] = (acc[h] + own).astype(out_ref.dtype)
 
     def drain(b, carry):
         @pl.when((o < n - 1) & (b <= o))
@@ -284,7 +301,8 @@
 
         @pl.when(b != t)
         def _():
-            part_copy(b, t).wait_send()
+            part_copy(b, t, 0).wait_send()
+            part_copy(b, t, 1).wait_send()
 
         @pl.when(b != o)
         def _():
@@ -298,7 +316,8 @@
 
     @pl.when(o != t)
     def _():
-        swap_copy().wait_send()
+        swap_copy(0).wait_send()
+        swap_copy(1).wait_send()
 
 
 def fused(
@@ -309,22 +328,15 @@
     cols = output_weight.shape[1]
     bank, rank = adapter_down_bank.shape[0], adapter_down_bank.shape[2]
     cap = max(2, (2 * rows + n - 1) // n)
-    adapters = jnp.arange(adapter_position.shape[0], dtype=jnp.int32)
-    matched = request_adapter[:, None] == adapters[None, :]
-    position = jnp.sum(jnp.where(matched, adapter_position[None, :], 0), axis=1)
-    owner_of = position // bank
-    before = jnp.arange(rows)[None, :] < jnp.arange(rows)[:, None]
-    same = owner_of[:, None] == owner_of[None, :]
-    target = owner_of * cap + jnp.sum(same & before, axis=-1)
-    meta = jnp.where(jnp.arange(2 * LANES)[None, :] < LANES, position[:, None], target[:, None]).astype(BF16)
     down = jnp.swapaxes(adapter_down_bank, 1, 2).reshape(bank * rank, width)
     up = adapter_up_bank.reshape(bank * rank, cols)
+    vmem = pl.BlockSpec(memory_space=pltpu.VMEM)
     anywhere = pl.BlockSpec(memory_space=pl.ANY)
     dma = pltpu.SemaphoreType.DMA
     return pl.pallas_call(
         functools.partial(kernel, n, bank, rank, cap, 512),
         out_shape=jax.ShapeDtypeStruct((rows, cols), BF16),
-        in_specs=[anywhere] * 5,
+        in_specs=[anywhere, vmem, vmem, anywhere, anywhere, anywhere],
         out_specs=pl.BlockSpec(memory_space=pltpu.VMEM),
         scratch_shapes=[
             pltpu.VMEM((n, rows, width + 2 * LANES), BF16),
@@ -332,20 +344,20 @@
             pltpu.VMEM((bank * rank, width), BF16),
             pltpu.VMEM((bank * rank, cols), BF16),
             pltpu.VMEM((n, n, rows, LANES), F32),
-            pltpu.VMEM((n, rows, cols), BF16),
-            pltpu.VMEM((n, rows, cols), BF16),
-            pltpu.VMEM((rows, cols), F32),
-            pltpu.VMEM((rows, cols), BF16),
-            pltpu.VMEM((rows, cols), BF16),
+            pltpu.VMEM((n, 2, rows, cols // 2), BF16),
+            pltpu.VMEM((n, 2, rows, cols // 2), BF16),
+            pltpu.VMEM((2, rows, cols // 2), F32),
+            pltpu.VMEM((2, rows, cols // 2), BF16),
+            pltpu.VMEM((2, rows, cols // 2), BF16),
             pltpu.VMEM((n, 2 * cap, cols // 2), BF16),
             pltpu.VMEM((n * 2 * cap, cols // 2), BF16),
-            dma((5,)), dma((n,)), dma((n,)), dma((n,)), dma((n, n)), dma((n, n)), dma((n,)), dma((n,)),
-            dma((n,)), dma((n,)), dma, dma,
+            dma((4,)), dma((n,)), dma((n,)), dma((n,)), dma((n, n)), dma((n, n)), dma((n, 2)), dma((n, 2)),
+            dma((n,)), dma((n,)), dma((2,)), dma((2,)),
         ],
         compiler_params=pltpu.CompilerParams(
             collective_id=0, has_side_effects=True, vmem_limit_bytes=60 * 2**20
         ),
-    )(requests, meta, output_weight, down, up)
+    )(requests, request_adapter[None], adapter_position[None], output_weight, down, up)
 
 
 def shards(
@@ -360,13 +372,14 @@
     cap = max(2, (2 * rows + owners - 1) // owners)
     fits = (
         owners == pieces
-        and output_weight.shape[1] % 512 == 0
+        and output_weight.shape[1] % 1024 == 0
         and 2 * rank == LANES
         and bank * rank % LANES == 0
         and rows % 16 == 0
         and cap % 8 == 0
         and cap <= LANES
         and owners * max(bank, cap) <= 256
+        and adapter_position.shape[0] <= owners * bank
     )
     return fused(*arguments) if fits else general(*arguments)
 

time: 52 us -> 45.9 us (0.88)
  the two profiles are of different devices: /device:TPU:7 before, /device:TPU:6 now
where the time goes in v2:
time: 45.9 us; the launch traced here: 45.8 us
  Pallas kernels  44.2 us (96%)
  local copies, waits for them, and re-layouts  1.62 us (4%)
    pallas_call x1, Pallas kernels, fused(): pl.pallas_call(functools.partial(kernel, n, bank, rank, cap, 512), out_sh...  44.2 us
    unnamed x1, local copies, waits for them, and re-layouts  1.62 us

profile of v2, /device:TPU:6, one launch (start us, length us, event | category | flops | bytes accessed | tf_op | source)
XLA Modules:
  0.0 45.8 jit_solution(11928992659105491900)
XLA Ops:
  0.0 44.2 %shard_map.64 = bf16[48,2048]{1,0:T(8,128)(2,1)} custom-call(bf16[48,2048]{1,0:T(8,128)(2,1)} %x_hbm.1, s32[1,48]{1,0:T(1,128)} %bitcast.8, s32[1,24]{1,0:T(1,128)} %bitcast.9, bf16[2048,2048]{1,0:T(8,128)(2,1)} %w_hbm.1, bf16[384,2048]{1,0:T(8,128)(2,1)} %bitcast.6, bf16[384,2048]{1,0:T(8,128)(2,1)} %bitcast.7), custom_call_target="tpu_custom_call" | custom-call | tf_op jit(solution)/shard_map/pallas_call | solution.py:336
  44.2 1.6 %copy.8 = bf16[48,2048]{1,0:T(8,128)(2,1)} copy(bf16[48,2048]{1,0:T(8,128)(2,1)} %shard_map.64) | data formatting | bytes 393216

commit v3 on v2

--- a/solution.py
+++ b/solution.py
@@ -180,67 +180,15 @@
             def _():
                 swap_copy(h).start()
 
-    def block(k, carry):
-        b = order(k)
-
-        below, above = jnp.maximum(o - k, 0), jnp.minimum(o + k, n - 1)
-
-        @pl.when((k > 0) & (o - k >= 0))
-        def _():
-            x_up(below).wait_recv()
-
-        @pl.when((o < n - 1) & (o - k >= 0))
-        def _():
-            x_up(below).start()
-
-        @pl.when((k > 0) & (o + k < n))
-        def _():
-            x_up(above).wait_recv()
-
-        @pl.when((o > 0) & (o + k < n))
-        def _():
-            x_down(above).start()
-
-        @pl.when(k == 0)
-        def _():
-            loads[1].wait()
-
+    def routes(b):
         place = xg[b, :, width : width + LANES].astype(F32)
         target = xg[b, :, width + LANES : width + 2 * LANES].astype(F32)
         lane = lax.broadcasted_iota(jnp.int32, (rows, bank * rank), 1)
         mine = jnp.concatenate([place] * copies, axis=1) == (lane // rank + o * bank).astype(F32)
-        every = jnp.where(mine, dot(xg[b, :, :width], down[...], ((1,), (1,))), 0.0)
-        folded = every[:, :LANES]
-        for i in range(1, copies):
-            folded += every[:, i * LANES : (i + 1) * LANES]
-        low[b, t] = folded + pltpu.roll(folded, rank, 1)
-        for s in range(1, n):
-            low_copy(b, lax.rem(t + s, n), t).start()
-
-        @pl.when(k == 0)
-        def _():
-            loads[2].wait()
-
-        for h in range(2):
-
-            @pl.loop(0, half // tile)
-            def _(c):
-                at = pl.ds(pl.multiple_of(c * tile, tile), tile)
-                value = dot(xg[b, :, :width], w[:, pl.ds(pl.multiple_of(h * half + c * tile, tile), tile)])
-                part[b, h, :, at] = value.astype(BF16)
-
-                @pl.when(b == t)
-                def _():
-                    acc[h, :, at] = value
-
-            @pl.when(b != t)
-            def _():
-                part_copy(b, t, h).start()
-
-        @pl.when(k == 0)
-        def _():
-            loads[3].wait()
-
+        return mine, target
+
+    def finish_low(b):
+        mine, target = routes(b)
         for s in range(1, n):
             low_copy(b, t, lax.rem(t + s, n)).wait_recv()
         total = low[b, 0]
@@ -261,6 +209,66 @@
             delta_out[b] = made
             delta_copy(b, o).start()
 
+
+    def block(k, carry):
+        b = order(k)
+
+        below, above = jnp.maximum(o - k, 0), jnp.minimum(o + k, n - 1)
+
+        @pl.when((k > 0) & (o - k >= 0))
+        def _():
+            x_up(below).wait_recv()
+
+        @pl.when((o < n - 1) & (o - k >= 0))
+        def _():
+            x_up(below).start()
+
+        @pl.when((k > 0) & (o + k < n))
+        def _():
+            x_up(above).wait_recv()
+
+        @pl.when((o > 0) & (o + k < n))
+        def _():
+            x_down(above).start()
+
+        @pl.when(k == 0)
+        def _():
+            loads[1].wait()
+            loads[3].wait()
+
+        @pl.when(k > 0)
+        def _():
+            finish_low(order(jnp.maximum(k - 1, 0)))
+
+        mine, _ = routes(b)
+        every = jnp.where(mine, dot(xg[b, :, :width], down[...], ((1,), (1,))), 0.0)
+        folded = every[:, :LANES]
+        for i in range(1, copies):
+            folded += every[:, i * LANES : (i + 1) * LANES]
+        low[b, t] = folded + pltpu.roll(folded, rank, 1)
+        for s in range(1, n):
+            low_copy(b, lax.rem(t + s, n), t).start()
+
+        @pl.when(k == 0)
+        def _():
+            loads[2].wait()
+
+        for h in range(2):
+
+            @pl.loop(0, half // tile)
+            def _(c):
+                at = pl.ds(pl.multiple_of(c * tile, tile), tile)
+                value = dot(xg[b, :, :width], w[:, pl.ds(pl.multiple_of(h * half + c * tile, tile), tile)])
+                part[b, h, :, at] = value.astype(BF16)
+
+                @pl.when(b == t)
+                def _():
+                    acc[h, :, at] = value
+
+            @pl.when(b != t)
+            def _():
+                part_copy(b, t, h).start()
+
         @pl.when((k > 0) & (order(jnp.maximum(k - 1, 0)) == t))
         def _():
             finish_parts()
@@ -268,6 +276,7 @@
         return carry
 
     lax.fori_loop(0, n, block, 0)
+    finish_low(order(n - 1))
 
     @pl.when(order(n - 1) == t)
     def _():

time: 45.9 us -> 45 us (0.980)
  the two profiles are of different devices: /device:TPU:6 before, /device:TPU:1 now
where the time goes in v3:
time: 45 us; the launch traced here: 44.9 us
  Pallas kernels  43.2 us (96%)
  local copies, waits for them, and re-layouts  1.62 us (4%)
    pallas_call x1, Pallas kernels, fused(): pl.pallas_call(functools.partial(kernel, n, bank, rank, cap, 512), out_sh...  43.2 us
    unnamed x1, local copies, waits for them, and re-layouts  1.62 us

profile of v3, /device:TPU:1, one launch (start us, length us, event | category | flops | bytes accessed | tf_op | source)
XLA Modules:
  0.0 44.9 jit_solution(4759517302483728240)
XLA Ops:
  0.0 43.2 %shard_map.64 = bf16[48,2048]{1,0:T(8,128)(2,1)} custom-call(bf16[48,2048]{1,0:T(8,128)(2,1)} %x_hbm.1, s32[1,48]{1,0:T(1,128)} %bitcast.8, s32[1,24]{1,0:T(1,128)} %bitcast.9, bf16[2048,2048]{1,0:T(8,128)(2,1)} %w_hbm.1, bf16[384,2048]{1,0:T(8,128)(2,1)} %bitcast.6, bf16[384,2048]{1,0:T(8,128)(2,1)} %bitcast.7), custom_call_target="tpu_custom_call" | custom-call | tf_op jit(solution)/shard_map/pallas_call | solution.py:345
  43.2 1.6 %copy.8 = bf16[48,2048]{1,0:T(8,128)(2,1)} copy(bf16[48,2048]{1,0:T(8,128)(2,1)} %shard_map.64) | data formatting | bytes 393216
